TPU v7x, 32 devices: a whole 2x2x4 slice. The times are simulated.
32 devices in a mesh: gx: 8 (over y, x, core), gy: 4 (over z).
Axes of the slice: x: 2, y: 2, z: 4, core: 2. Of those that a mesh axis runs over, the one named last changes fastest.
Arguments:
- wave_state: float32 [3, 128, 512, 128], P(None, 'gy', 'gx'), may hold values from -6 to 6
- tracers: float32 [6, 128, 512, 128], P(None, 'gy', 'gx'), may hold values from -6 to 6
- eddy: float32 [128, 512, 128], P('gy', 'gx'), may hold values from 0.05 to 2
- cost_class: int32 [128, 512], P('gy', 'gx'), may hold values from 0 to 3
- span_slot: int32 [128, 512], P('gy', 'gx'), may hold values from 0 to 4095, as said below
Outputs:
- wave_after: float32 [3, 128, 512, 128], P(None, 'gy', 'gx')
- tracers_after: float32 [6, 128, 512, 128], P(None, 'gy', 'gx')
- span_tendency: float32 [32, 32, 128, 128], P(('gx', 'gy'))
Inputs may be any that keep to these rules, and one draw needn't show every extreme that they name: span_slot is owner * 128 + slot, with owner an index along gx+gy and slot below 128; among the columns of one device no two hold the same value; every owner receives all 128 slots from at least one device.
All inputs are finite; a program needn't handle non-finite values.
Results may differ from a plain program's by a relative error of at most 0.00002.
Values sent between devices are 32-bit elements; how exact they have to be, the bound alone decides.
A program may use at most 192 MiB of HBM per device.

v0:
```python
import jax
import jax.numpy as jnp
from jax import lax
from jax.sharding import PartitionSpec as P

SUBSTEPS = 4


COURANT = 0.6


def extended(block, sides, width, periodic):
    for axis, dim in sides:
        count = lax.axis_size(axis)
        forward = [(i, i + 1) for i in range(count - 1)]
        if periodic:
            forward.append((count - 1, 0))
        backward = [(target, source) for source, target in forward]
        low = lax.ppermute(
            lax.slice_in_dim(block, block.shape[dim] - width, None, axis=dim), axis, forward
        )
        high = lax.ppermute(lax.slice_in_dim(block, 0, width, axis=dim), axis, backward)
        block = jnp.concatenate([low, block, high], axis=dim)
    return block


def wave_step(padded):
    press = padded[0]
    east = padded[1]
    north = padded[2]
    east_new = east[:, :-1] - COURANT * (press[:, 1:] - press[:, :-1])
    north_new = north[:-1, :] - COURANT * (press[1:, :] - press[:-1, :])
    press_new = press[1:-1, 1:-1] - COURANT * (
        east_new[1:-1, 1:] - east_new[1:-1, :-1] + (north_new[1:, 1:-1] - north_new[:-1, 1:-1])
    )
    return jnp.stack([press_new, east_new[1:-1, 1:], north_new[1:, 1:-1]])


def shear_factor(wave):
    east = wave[1]
    north = wave[2]
    shear = jnp.abs(east[:, :, 1:] - east[:, :, :-1]) + jnp.abs(north[:, :, 1:] - north[:, :, :-1])
    shear = jnp.concatenate([shear, jnp.zeros_like(shear[:, :, :1])], axis=2)
    return 1.0 + shear


def column_solve(mixing_rows, tracer_rows):
    mixing = mixing_rows.T
    rhs_levels = jnp.transpose(tracer_rows, (2, 0, 1))
    level_count = mixing.shape[0]
    zero_row = jnp.zeros_like(mixing[0])
    c_prev = zero_row
    d_prev = jnp.zeros_like(rhs_levels[0])
    coeffs = []
    values = []
    for level in range(level_count):
        lower = mixing[level - 1] if level > 0 else zero_row
        upper = mixing[level] if level < level_count - 1 else zero_row
        middle = 1.0 + lower + upper
        denom = middle + lower * c_prev
        c_now = -upper / denom
        d_now = (rhs_levels[level] + lower[None] * d_prev) / denom[None]
        coeffs.append(c_now)
        values.append(d_now)
        c_prev = c_now
        d_prev = d_now
    x_next = jnp.zeros_like(rhs_levels[0])
    solved = [None] * level_count
    for level in range(level_count - 1, -1, -1):
        x_now = values[level] - coeffs[level][None] * x_next
        solved[level] = x_now
        x_next = x_now
    return jnp.stack(solved, axis=2)


def implicit_mix(mixing_rows, tracer_rows):
    row_count, levels = mixing_rows.shape
    tracer_count = tracer_rows.shape[0]
    block_rows = min(512, row_count & -row_count)
    block_count = row_count // block_rows
    mix_blocks = mixing_rows.reshape(block_count, block_rows, levels)
    tracer_blocks = jnp.transpose(
        tracer_rows.reshape(tracer_count, block_count, block_rows, levels), (1, 0, 2, 3)
    )
    solved = lax.map(lambda pair: column_solve(pair[0], pair[1]), (mix_blocks, tracer_blocks))
    return jnp.transpose(solved, (1, 0, 2, 3)).reshape(tracer_count, row_count, levels)


def advance(wave, depth):
    rows_total = wave.shape[1] * lax.axis_size("gy")
    first_row = lax.axis_index("gy") * wave.shape[1]
    for group in range(SUBSTEPS // depth):
        padded = extended(wave, (("gx", 2),), depth, True)
        padded = extended(padded, (("gy", 1),), depth, False)
        padded = wave_step(padded)
        margin = depth - 1
        row_ids = first_row - margin + jnp.arange(padded.shape[1], dtype=jnp.int32)
        inside = ((row_ids >= 0) & (row_ids < rows_total)).astype(padded.dtype)
        padded = padded * inside[None, :, None, None]
        wave = padded
    return wave


def per_device(wave_state, tracers, eddy, cost_class, span_slot):
    wave_after = advance(wave_state, 1)
    lat_rows, lon_cols, levels = eddy.shape
    columns = lat_rows * lon_cols
    devices = lax.axis_size(("gx", "gy"))
    capacity = max(2, (2 * columns + devices - 1) // devices)
    tracer_count = tracers.shape[0]
    mixing = eddy * (1.0 + cost_class.astype(eddy.dtype))[:, :, None] * shear_factor(wave_after)
    mixing_rows = mixing.reshape(columns, levels)
    tracer_rows = tracers.reshape(tracer_count, columns, levels)
    targets = span_slot.reshape(columns)
    solved = implicit_mix(mixing_rows, tracer_rows)
    change = jnp.sum(solved - tracer_rows, axis=0)
    outgoing = jnp.zeros((devices * capacity, levels), change.dtype).at[targets].set(change)
    arrived = lax.all_to_all(
        outgoing.reshape(devices, capacity, levels),
        ("gx", "gy"),
        split_axis=0,
        concat_axis=0,
        tiled=True,
    )
    span = arrived[None]
    tracers_after = solved.reshape(tracer_count, lat_rows, lon_cols, levels)
    return (wave_after, tracers_after, span)


def solution(mesh):
    in_specs = (
        P(None, "gy", "gx", None),
        P(None, "gy", "gx", None),
        P("gy", "gx", None),
        P("gy", "gx"),
        P("gy", "gx"),
    )
    out_specs = (
        P(None, "gy", "gx", None),
        P(None, "gy", "gx", None),
        P(("gx", "gy"), None, None, None),
    )
    return jax.shard_map(
        per_device, mesh=mesh, in_specs=in_specs, out_specs=out_specs, check_vma=False
    )
```

profile of v0, /device:TPU:1, one launch (start us, length us, event | category | flops | bytes accessed | tf_op | source)
XLA Modules:
  0.0 445.2 jit_solution(8998756162426340444)
XLA Ops:
  0.6 1.3 fusion.378
  2.0 2.7 collective-permute-start
  5.8 2.3 collective-permute-done.1
  9.1 3.2 collective-permute-start.2
  12.3 1.3 collective-permute-start.3
  14.9 3.9 collective-permute-done.3
  22.7 2.3 collective-permute-done.5
  25.0 3.2 collective-permute-start.6
  28.2 1.3 collective-permute-start.7
  30.0 3.8 collective-permute-done.7
  35.8 1.8 collective-permute-start.8
  39.4 2.3 collective-permute-done.9
  42.4 3.2 collective-permute-start.10
  45.6 1.3 collective-permute-start.11
  47.7 3.7 collective-permute-done.11
  53.4 1.9 collective-permute-start.12
  56.9 2.4 collective-permute-done.13
  60.0 1.9 collective-permute-start.14
  61.9 1.3 collective-permute-start.15
  64.0 3.7 collective-permute-done.15
  70.0 1.4 copy-done.2
  72.9 306.2 %while.10 = (s32[]{:T(128)}, f32[4,6,512,128]{3,2,0,1:T(8,128)}, f32[4,6,512,128]{3,2,0,1:T(8,128)}, f32[4,512,128]{2,1,0:T(8,128)S(1)}, s32[]{:T(128)}) while((s32[]{:T(128)}, f32[4,6,512,128]{3,2,0,1:T(8,128)}, f32[4,6,512,128]{3,2,0,1:T(8,128)}, f32[4,512,128]{2,1,0:T(8,128)S(1)}, s32[]{:T(128)}) %tuple.571), condition=%wide.region_1.2_spmd, body=%wide.region_0.1_spmd.sunk | while | flops 3430401 | bytes 33918004 | solution.py:85
  82.7 1.3 negate_divide_fusion.268
  85.3 1.3 negate_divide_fusion.270
  87.9 1.3 negate_divide_fusion.272
  90.4 1.3 negate_divide_fusion.274
  118.0 2.7 constant_dynamic-slice_fusion.5
  120.6 2.1 copy.150
  124.1 6.6 %multiply_subtract_fusion.189 = (f32[6,512]{1,0:T(8,128)S(1)}, f32[6,512]{1,0:T(8,128)S(1)}, f32[6,512]{1,0:T(8,128)S(1)}, f32[6,512]{1,0:T(8,128)S(1)}, f32[6,5...) fusion(f32[512]{0:T(512)} %negate_divide_fusion.284, ...), kind=kLoop, calls=%fused_computation.611.clone.1 | loop fusion | flops 1198080 | bytes 2738176 | tf_op jit(solution)/shard_map/while/body/eval_jaxpr/sub | solution.py:70
  131.7 2.0 constant_dynamic-update-slice_fusion.258
  145.2 1.3 copy-done
  146.5 1.8 copy.151
  159.2 1.3 negate_divide_fusion.268
  161.8 1.3 negate_divide_fusion.270
  164.4 1.3 negate_divide_fusion.272
  166.9 1.3 negate_divide_fusion.274
  194.4 2.7 constant_dynamic-slice_fusion.5
  197.1 2.1 copy.150
  200.6 6.6 %multiply_subtract_fusion.189 = (f32[6,512]{1,0:T(8,128)S(1)}, f32[6,512]{1,0:T(8,128)S(1)}, f32[6,512]{1,0:T(8,128)S(1)}, f32[6,512]{1,0:T(8,128)S(1)}, f32[6,5...) fusion(f32[512]{0:T(512)} %negate_divide_fusion.284, ...), kind=kLoop, calls=%fused_computation.611.clone.1 | loop fusion | flops 1198080 | bytes 2738176 | tf_op jit(solution)/shard_map/while/body/eval_jaxpr/sub | solution.py:70
  208.2 2.0 constant_dynamic-update-slice_fusion.258
  221.7 1.3 copy-done
  223.0 1.8 copy.151
  235.7 1.3 negate_divide_fusion.268
  238.3 1.3 negate_divide_fusion.270
  243.4 1.3 negate_divide_fusion.274
  270.9 2.7 constant_dynamic-slice_fusion.5
  273.6 2.1 copy.150
  277.1 6.6 %multiply_subtract_fusion.189 = (f32[6,512]{1,0:T(8,128)S(1)}, f32[6,512]{1,0:T(8,128)S(1)}, f32[6,512]{1,0:T(8,128)S(1)}, f32[6,512]{1,0:T(8,128)S(1)}, f32[6,5...) fusion(f32[512]{0:T(512)} %negate_divide_fusion.284, ...), kind=kLoop, calls=%fused_computation.611.clone.1 | loop fusion | flops 1198080 | bytes 2738176 | tf_op jit(solution)/shard_map/while/body/eval_jaxpr/sub | solution.py:70
  284.7 2.0 constant_dynamic-update-slice_fusion.258
  298.2 1.3 copy-done
  299.5 1.8 copy.151
  312.2 1.3 negate_divide_fusion.268
  314.8 1.3 negate_divide_fusion.270
  319.9 1.3 negate_divide_fusion.274
  347.4 2.7 constant_dynamic-slice_fusion.5
  350.1 2.1 copy.150
  353.6 6.6 %multiply_subtract_fusion.189 = (f32[6,512]{1,0:T(8,128)S(1)}, f32[6,512]{1,0:T(8,128)S(1)}, f32[6,512]{1,0:T(8,128)S(1)}, f32[6,512]{1,0:T(8,128)S(1)}, f32[6,5...) fusion(f32[512]{0:T(512)} %negate_divide_fusion.284, ...), kind=kLoop, calls=%fused_computation.611.clone.1 | loop fusion | flops 1198080 | bytes 2738176 | tf_op jit(solution)/shard_map/while/body/eval_jaxpr/sub | solution.py:70
  361.2 2.0 constant_dynamic-update-slice_fusion.258
  374.7 1.3 copy-done
  376.0 1.8 copy.151
  379.1 5.4 %fusion.256 = f32[4,512,128]{2,1,0:T(8,128)S(1)} fusion(f32[4,6,512,128]{3,2,0,1:T(8,128)} %get-tuple-element.25, f32[6,4,512,128]{3,2,1,0:T(8,128)} %bitcast.2482), kind=kLoop, calls=%fused_computation.899 | loop fusion | flops 2883584 | bytes 13631488 | tf_op jit(solution)/shard_map/reduce_sum | solution.py:116
  384.5 6.2 %scatter_custom_fusion = f32[4096,128]{1,0:T(8,128)S(1)} fusion(s32[2048]{0:T(1024)} %bitcast.3006, f32[2048,128]{1,0:T(8,128)S(1)} %bitcast.2600, f32[]{:T(128)} %constant.25.clone.1), kind=kCustom, calls=%fused_computation.1011 | custom fusion | bytes 2097664 | tf_op jit(solution)/shard_map/scatter | solution.py:117
  390.7 53.1 %all_to_all.5 = f32[32,128,128]{2,1,0:T(8,128)S(1)} all-to-all(f32[32,128,128]{2,1,0:T(8,128)S(1)} %bitcast.2483), channel_id=1, replica_groups=mesh['gx'=8,'gy'=4] {'gx','gy'}, dimensions={0} | all-to-all | bytes 4194304 | tf_op jit(solution)/shard_map/all_to_all | solution.py:118
  443.8 1.3 copy.289
  (2247 shorter events, 230.7 us)
Async XLA Ops:
  2.0 3.8 collective-permute-start
  4.6 3.5 collective-permute-start.1
  9.1 5.8 %collective-permute-start.2 = (f32[3,1,66,128]{3,2,1,0:T(8,128)S(1)}, f32[3,1,66,128]{3,2,1,0:T(8,128)S(1)}, u32[]{:S(2)}, u32[]{:S(2)}) collective-permute-start(f32[3,1,66,128]{3,2,1,0:T(8,128)S(1)} %get-tuple-element.524), channel_id=1, source_target_pairs={{0,1},{1,2},{2,3},{4,5},{5,6},{6,7},{8,9},{9,10},{10,11},{12,13},{... | collective-permute-start | bytes 304136 | tf_op jit(solution)/shard_map/ppermute | solution.py:19
  12.3 6.5 %collective-permute-start.3 = (f32[3,1,66,128]{3,2,1,0:T(8,128)S(1)}, f32[3,1,66,128]{3,2,1,0:T(8,128)S(1)}, u32[]{:S(2)}, u32[]{:S(2)}) collective-permute-start(f32[3,1,66,128]{3,2,1,0:T(8,128)S(1)} %get-tuple-element.523), channel_id=1, source_target_pairs={{1,0},{2,1},{3,2},{5,4},{6,5},{7,6},{9,8},{10,9},{11,10},{13,12},{... | collective-permute-start | bytes 304136 | tf_op jit(solution)/shard_map/ppermute | solution.py:22
  21.0 1.6 collective-permute-start.4
  21.5 3.5 collective-permute-start.5
  25.0 4.9 %collective-permute-start.6 = (f32[3,1,66,128]{3,2,1,0:T(8,128)S(1)}, f32[3,1,66,128]{3,2,1,0:T(8,128)S(1)}, u32[]{:S(2)}, u32[]{:S(2)}) collective-permute-start(f32[3,1,66,128]{3,2,1,0:T(8,128)S(1)} %get-tuple-element.522), channel_id=1, source_target_pairs={{0,1},{1,2},{2,3},{4,5},{5,6},{6,7},{8,9},{9,10},{10,11},{12,13},{... | collective-permute-start | bytes 304136 | tf_op jit(solution)/shard_map/ppermute | solution.py:19
  28.2 5.5 %collective-permute-start.7 = (f32[3,1,66,128]{3,2,1,0:T(8,128)S(1)}, f32[3,1,66,128]{3,2,1,0:T(8,128)S(1)}, u32[]{:S(2)}, u32[]{:S(2)}) collective-permute-start(f32[3,1,66,128]{3,2,1,0:T(8,128)S(1)} %get-tuple-element.521), channel_id=1, source_target_pairs={{1,0},{2,1},{3,2},{5,4},{6,5},{7,6},{9,8},{10,9},{11,10},{13,12},{... | collective-permute-start | bytes 304136 | tf_op jit(solution)/shard_map/ppermute | solution.py:22
  35.8 3.6 collective-permute-start.8
  37.7 4.0 collective-permute-start.9
  42.4 5.2 %collective-permute-start.10 = (f32[3,1,66,128]{3,2,1,0:T(8,128)}, f32[3,1,66,128]{3,2,1,0:T(8,128)S(1)}, u32[]{:S(2)}, u32[]{:S(2)}) collective-permute-start(f32[3,1,66,128]{3,2,1,0:T(8,128)} %get-tuple-element.520), channel_id=1, source_target_pairs={{0,1},{1,2},{2,3},{4,5},{5,6},{6,7},{8,9},{9,10},{10,11},{12,13},{... | collective-permute-start | bytes 304136 | tf_op jit(solution)/shard_map/ppermute | solution.py:19
  45.6 5.7 %collective-permute-start.11 = (f32[3,1,66,128]{3,2,1,0:T(8,128)}, f32[3,1,66,128]{3,2,1,0:T(8,128)S(1)}, u32[]{:S(2)}, u32[]{:S(2)}) collective-permute-start(f32[3,1,66,128]{3,2,1,0:T(8,128)} %get-tuple-element.519), channel_id=1, source_target_pairs={{1,0},{2,1},{3,2},{5,4},{6,5},{7,6},{9,8},{10,9},{11,10},{13,12},{... | collective-permute-start | bytes 304136 | tf_op jit(solution)/shard_map/ppermute | solution.py:22
  53.4 3.6 collective-permute-start.12
  55.3 4.0 collective-permute-start.13
  60.0 4.0 collective-permute-start.14
  61.9 5.7 %collective-permute-start.15 = (f32[3,1,66,128]{3,2,1,0:T(8,128)}, f32[3,1,66,128]{3,2,1,0:T(8,128)S(1)}, u32[]{:S(2)}, u32[]{:S(2)}) collective-permute-start(f32[3,1,66,128]{3,2,1,0:T(8,128)} %get-tuple-element.517), channel_id=1, source_target_pairs={{1,0},{2,1},{3,2},{5,4},{6,5},{7,6},{9,8},{10,9},{11,10},{13,12},{... | collective-permute-start | bytes 304136 | tf_op jit(solution)/shard_map/ppermute | solution.py:22
  73.5 28.4 %copy-start.4 = (f32[1,512]{1,0:T(1,128)}, f32[1,512]{1,0:T(1,128)S(1)}, u32[]{:S(2)}) copy-start(f32[1,512]{1,0:T(1,128)S(1)} %get-tuple-element.1167) | copy-start | bytes 6148 | tf_op jit(solution)/shard_map/while
  73.5 28.3 %copy-start.76 = (f32[1,512]{1,0:T(1,128)}, f32[1,512]{1,0:T(1,128)S(1)}, u32[]{:S(2)}) copy-start(f32[1,512]{1,0:T(1,128)S(1)} %get-tuple-element.1170) | copy-start | bytes 6148 | tf_op jit(solution)/shard_map/while
  73.5 28.3 %copy-start.77 = (f32[1,512]{1,0:T(1,128)}, f32[1,512]{1,0:T(1,128)S(1)}, u32[]{:S(2)}) copy-start(f32[1,512]{1,0:T(1,128)S(1)} %get-tuple-element.1172) | copy-start | bytes 6148 | tf_op jit(solution)/shard_map/while
  73.6 28.3 %copy-start.78 = (f32[1,512]{1,0:T(1,128)}, f32[1,512]{1,0:T(1,128)S(1)}, u32[]{:S(2)}) copy-start(f32[1,512]{1,0:T(1,128)S(1)} %get-tuple-element.1174) | copy-start | bytes 6148 | tf_op jit(solution)/shard_map/while
  73.6 28.3 %copy-start.79 = (f32[1,512]{1,0:T(1,128)}, f32[1,512]{1,0:T(1,128)S(1)}, u32[]{:S(2)}) copy-start(f32[1,512]{1,0:T(1,128)S(1)} %get-tuple-element.1176) | copy-start | bytes 6148 | tf_op jit(solution)/shard_map/while
  73.6 34.0 %copy-start.14 = (f32[1,512]{1,0:T(1,128)}, f32[1,512]{1,0:T(1,128)S(1)}, u32[]{:S(2)}) copy-start(f32[1,512]{1,0:T(1,128)S(1)} %get-tuple-element.1177) | copy-start | bytes 6148 | tf_op jit(solution)/shard_map/while
  73.6 34.0 %copy-start.16 = (f32[1,512]{1,0:T(1,128)}, f32[1,512]{1,0:T(1,128)S(1)}, u32[]{:S(2)}) copy-start(f32[1,512]{1,0:T(1,128)S(1)} %get-tuple-element.1044) | copy-start | bytes 6148 | tf_op jit(solution)/shard_map/while
  73.7 28.2 %copy-start.80 = (f32[1,512]{1,0:T(1,128)}, f32[1,512]{1,0:T(1,128)S(1)}, u32[]{:S(2)}) copy-start(f32[1,512]{1,0:T(1,128)S(1)} %get-tuple-element.1180) | copy-start | bytes 6148 | tf_op jit(solution)/shard_map/while
  75.4 26.5 %copy-start.81 = (f32[512]{0:T(512)}, f32[512]{0:T(512)S(1)}, u32[]{:S(2)}) copy-start(f32[512]{0:T(512)S(1)} %get-tuple-element.1182) | copy-start | bytes 6148 | tf_op jit(solution)/shard_map/while
  76.0 25.9 %copy-start.82 = (f32[512]{0:T(512)}, f32[512]{0:T(512)S(1)}, u32[]{:S(2)}) copy-start(f32[512]{0:T(512)S(1)} %get-tuple-element.1183) | copy-start | bytes 6148 | tf_op jit(solution)/shard_map/while
  76.6 25.3 %copy-start.83 = (f32[512]{0:T(512)}, f32[512]{0:T(512)S(1)}, u32[]{:S(2)}) copy-start(f32[512]{0:T(512)S(1)} %get-tuple-element.1184) | copy-start | bytes 6148 | tf_op jit(solution)/shard_map/while
  77.2 24.7 %copy-start.84 = (f32[512]{0:T(512)}, f32[512]{0:T(512)S(1)}, u32[]{:S(2)}) copy-start(f32[512]{0:T(512)S(1)} %get-tuple-element.1185) | copy-start | bytes 6148 | tf_op jit(solution)/shard_map/while
  150.0 28.4 %copy-start.4 = (f32[1,512]{1,0:T(1,128)}, f32[1,512]{1,0:T(1,128)S(1)}, u32[]{:S(2)}) copy-start(f32[1,512]{1,0:T(1,128)S(1)} %get-tuple-element.1167) | copy-start | bytes 6148 | tf_op jit(solution)/shard_map/while
  150.0 28.3 %copy-start.76 = (f32[1,512]{1,0:T(1,128)}, f32[1,512]{1,0:T(1,128)S(1)}, u32[]{:S(2)}) copy-start(f32[1,512]{1,0:T(1,128)S(1)} %get-tuple-element.1170) | copy-start | bytes 6148 | tf_op jit(solution)/shard_map/while
  150.0 28.3 %copy-start.77 = (f32[1,512]{1,0:T(1,128)}, f32[1,512]{1,0:T(1,128)S(1)}, u32[]{:S(2)}) copy-start(f32[1,512]{1,0:T(1,128)S(1)} %get-tuple-element.1172) | copy-start | bytes 6148 | tf_op jit(solution)/shard_map/while
  150.1 28.3 %copy-start.78 = (f32[1,512]{1,0:T(1,128)}, f32[1,512]{1,0:T(1,128)S(1)}, u32[]{:S(2)}) copy-start(f32[1,512]{1,0:T(1,128)S(1)} %get-tuple-element.1174) | copy-start | bytes 6148 | tf_op jit(solution)/shard_map/while
  150.1 28.3 %copy-start.79 = (f32[1,512]{1,0:T(1,128)}, f32[1,512]{1,0:T(1,128)S(1)}, u32[]{:S(2)}) copy-start(f32[1,512]{1,0:T(1,128)S(1)} %get-tuple-element.1176) | copy-start | bytes 6148 | tf_op jit(solution)/shard_map/while
  150.1 34.0 %copy-start.14 = (f32[1,512]{1,0:T(1,128)}, f32[1,512]{1,0:T(1,128)S(1)}, u32[]{:S(2)}) copy-start(f32[1,512]{1,0:T(1,128)S(1)} %get-tuple-element.1177) | copy-start | bytes 6148 | tf_op jit(solution)/shard_map/while
  150.1 34.0 %copy-start.16 = (f32[1,512]{1,0:T(1,128)}, f32[1,512]{1,0:T(1,128)S(1)}, u32[]{:S(2)}) copy-start(f32[1,512]{1,0:T(1,128)S(1)} %get-tuple-element.1044) | copy-start | bytes 6148 | tf_op jit(solution)/shard_map/while
  150.2 28.2 %copy-start.80 = (f32[1,512]{1,0:T(1,128)}, f32[1,512]{1,0:T(1,128)S(1)}, u32[]{:S(2)}) copy-start(f32[1,512]{1,0:T(1,128)S(1)} %get-tuple-element.1180) | copy-start | bytes 6148 | tf_op jit(solution)/shard_map/while
  151.9 26.5 %copy-start.81 = (f32[512]{0:T(512)}, f32[512]{0:T(512)S(1)}, u32[]{:S(2)}) copy-start(f32[512]{0:T(512)S(1)} %get-tuple-element.1182) | copy-start | bytes 6148 | tf_op jit(solution)/shard_map/while
  152.5 25.9 %copy-start.82 = (f32[512]{0:T(512)}, f32[512]{0:T(512)S(1)}, u32[]{:S(2)}) copy-start(f32[512]{0:T(512)S(1)} %get-tuple-element.1183) | copy-start | bytes 6148 | tf_op jit(solution)/shard_map/while
  153.1 25.3 %copy-start.83 = (f32[512]{0:T(512)}, f32[512]{0:T(512)S(1)}, u32[]{:S(2)}) copy-start(f32[512]{0:T(512)S(1)} %get-tuple-element.1184) | copy-start | bytes 6148 | tf_op jit(solution)/shard_map/while
  153.7 24.7 %copy-start.84 = (f32[512]{0:T(512)}, f32[512]{0:T(512)S(1)}, u32[]{:S(2)}) copy-start(f32[512]{0:T(512)S(1)} %get-tuple-element.1185) | copy-start | bytes 6148 | tf_op jit(solution)/shard_map/while
  226.5 28.4 %copy-start.4 = (f32[1,512]{1,0:T(1,128)}, f32[1,512]{1,0:T(1,128)S(1)}, u32[]{:S(2)}) copy-start(f32[1,512]{1,0:T(1,128)S(1)} %get-tuple-element.1167) | copy-start | bytes 6148 | tf_op jit(solution)/shard_map/while
  226.5 28.3 %copy-start.76 = (f32[1,512]{1,0:T(1,128)}, f32[1,512]{1,0:T(1,128)S(1)}, u32[]{:S(2)}) copy-start(f32[1,512]{1,0:T(1,128)S(1)} %get-tuple-element.1170) | copy-start | bytes 6148 | tf_op jit(solution)/shard_map/while
  226.5 28.3 %copy-start.77 = (f32[1,512]{1,0:T(1,128)}, f32[1,512]{1,0:T(1,128)S(1)}, u32[]{:S(2)}) copy-start(f32[1,512]{1,0:T(1,128)S(1)} %get-tuple-element.1172) | copy-start | bytes 6148 | tf_op jit(solution)/shard_map/while
  226.6 28.3 %copy-start.78 = (f32[1,512]{1,0:T(1,128)}, f32[1,512]{1,0:T(1,128)S(1)}, u32[]{:S(2)}) copy-start(f32[1,512]{1,0:T(1,128)S(1)} %get-tuple-element.1174) | copy-start | bytes 6148 | tf_op jit(solution)/shard_map/while
  226.6 28.3 %copy-start.79 = (f32[1,512]{1,0:T(1,128)}, f32[1,512]{1,0:T(1,128)S(1)}, u32[]{:S(2)}) copy-start(f32[1,512]{1,0:T(1,128)S(1)} %get-tuple-element.1176) | copy-start | bytes 6148 | tf_op jit(solution)/shard_map/while
  226.6 34.0 %copy-start.14 = (f32[1,512]{1,0:T(1,128)}, f32[1,512]{1,0:T(1,128)S(1)}, u32[]{:S(2)}) copy-start(f32[1,512]{1,0:T(1,128)S(1)} %get-tuple-element.1177) | copy-start | bytes 6148 | tf_op jit(solution)/shard_map/while
  226.6 34.0 %copy-start.16 = (f32[1,512]{1,0:T(1,128)}, f32[1,512]{1,0:T(1,128)S(1)}, u32[]{:S(2)}) copy-start(f32[1,512]{1,0:T(1,128)S(1)} %get-tuple-element.1044) | copy-start | bytes 6148 | tf_op jit(solution)/shard_map/while
  226.7 28.2 %copy-start.80 = (f32[1,512]{1,0:T(1,128)}, f32[1,512]{1,0:T(1,128)S(1)}, u32[]{:S(2)}) copy-start(f32[1,512]{1,0:T(1,128)S(1)} %get-tuple-element.1180) | copy-start | bytes 6148 | tf_op jit(solution)/shard_map/while
  228.4 26.5 %copy-start.81 = (f32[512]{0:T(512)}, f32[512]{0:T(512)S(1)}, u32[]{:S(2)}) copy-start(f32[512]{0:T(512)S(1)} %get-tuple-element.1182) | copy-start | bytes 6148 | tf_op jit(solution)/shard_map/while
  229.0 25.9 %copy-start.82 = (f32[512]{0:T(512)}, f32[512]{0:T(512)S(1)}, u32[]{:S(2)}) copy-start(f32[512]{0:T(512)S(1)} %get-tuple-element.1183) | copy-start | bytes 6148 | tf_op jit(solution)/shard_map/while
  229.6 25.3 %copy-start.83 = (f32[512]{0:T(512)}, f32[512]{0:T(512)S(1)}, u32[]{:S(2)}) copy-start(f32[512]{0:T(512)S(1)} %get-tuple-element.1184) | copy-start | bytes 6148 | tf_op jit(solution)/shard_map/while
  230.2 24.7 %copy-start.84 = (f32[512]{0:T(512)}, f32[512]{0:T(512)S(1)}, u32[]{:S(2)}) copy-start(f32[512]{0:T(512)S(1)} %get-tuple-element.1185) | copy-start | bytes 6148 | tf_op jit(solution)/shard_map/while
  303.0 28.4 %copy-start.4 = (f32[1,512]{1,0:T(1,128)}, f32[1,512]{1,0:T(1,128)S(1)}, u32[]{:S(2)}) copy-start(f32[1,512]{1,0:T(1,128)S(1)} %get-tuple-element.1167) | copy-start | bytes 6148 | tf_op jit(solution)/shard_map/while
  303.0 28.3 %copy-start.76 = (f32[1,512]{1,0:T(1,128)}, f32[1,512]{1,0:T(1,128)S(1)}, u32[]{:S(2)}) copy-start(f32[1,512]{1,0:T(1,128)S(1)} %get-tuple-element.1170) | copy-start | bytes 6148 | tf_op jit(solution)/shard_map/while
  303.0 28.3 %copy-start.77 = (f32[1,512]{1,0:T(1,128)}, f32[1,512]{1,0:T(1,128)S(1)}, u32[]{:S(2)}) copy-start(f32[1,512]{1,0:T(1,128)S(1)} %get-tuple-element.1172) | copy-start | bytes 6148 | tf_op jit(solution)/shard_map/while
  303.1 28.3 %copy-start.78 = (f32[1,512]{1,0:T(1,128)}, f32[1,512]{1,0:T(1,128)S(1)}, u32[]{:S(2)}) copy-start(f32[1,512]{1,0:T(1,128)S(1)} %get-tuple-element.1174) | copy-start | bytes 6148 | tf_op jit(solution)/shard_map/while
  303.1 28.3 %copy-start.79 = (f32[1,512]{1,0:T(1,128)}, f32[1,512]{1,0:T(1,128)S(1)}, u32[]{:S(2)}) copy-start(f32[1,512]{1,0:T(1,128)S(1)} %get-tuple-element.1176) | copy-start | bytes 6148 | tf_op jit(solution)/shard_map/while
  303.1 34.0 %copy-start.14 = (f32[1,512]{1,0:T(1,128)}, f32[1,512]{1,0:T(1,128)S(1)}, u32[]{:S(2)}) copy-start(f32[1,512]{1,0:T(1,128)S(1)} %get-tuple-element.1177) | copy-start | bytes 6148 | tf_op jit(solution)/shard_map/while
  303.1 34.0 %copy-start.16 = (f32[1,512]{1,0:T(1,128)}, f32[1,512]{1,0:T(1,128)S(1)}, u32[]{:S(2)}) copy-start(f32[1,512]{1,0:T(1,128)S(1)} %get-tuple-element.1044) | copy-start | bytes 6148 | tf_op jit(solution)/shard_map/while
  303.2 28.2 %copy-start.80 = (f32[1,512]{1,0:T(1,128)}, f32[1,512]{1,0:T(1,128)S(1)}, u32[]{:S(2)}) copy-start(f32[1,512]{1,0:T(1,128)S(1)} %get-tuple-element.1180) | copy-start | bytes 6148 | tf_op jit(solution)/shard_map/while
  304.9 26.5 %copy-start.81 = (f32[512]{0:T(512)}, f32[512]{0:T(512)S(1)}, u32[]{:S(2)}) copy-start(f32[512]{0:T(512)S(1)} %get-tuple-element.1182) | copy-start | bytes 6148 | tf_op jit(solution)/shard_map/while
  305.5 25.9 %copy-start.82 = (f32[512]{0:T(512)}, f32[512]{0:T(512)S(1)}, u32[]{:S(2)}) copy-start(f32[512]{0:T(512)S(1)} %get-tuple-element.1183) | copy-start | bytes 6148 | tf_op jit(solution)/shard_map/while
  306.1 25.3 %copy-start.83 = (f32[512]{0:T(512)}, f32[512]{0:T(512)S(1)}, u32[]{:S(2)}) copy-start(f32[512]{0:T(512)S(1)} %get-tuple-element.1184) | copy-start | bytes 6148 | tf_op jit(solution)/shard_map/while
  306.7 24.7 %copy-start.84 = (f32[512]{0:T(512)}, f32[512]{0:T(512)S(1)}, u32[]{:S(2)}) copy-start(f32[512]{0:T(512)S(1)} %get-tuple-element.1185) | copy-start | bytes 6148 | tf_op jit(solution)/shard_map/while
  (613 other events, 6998.0 us)
where the time goes:
time: 449 us; the launch traced here: 445 us
  other arithmetic  269 us (60%)
  local copies, waits for them, and re-layouts  53.1 us (12%)
  blocking collectives  53.1 us (12%)
  waiting for transfers between devices  30 us (7%)
  starting transfers between devices  26.1 us (6%)
  loops' own time  13.1 us (3%)
    div x340, other arithmetic, column_solve(): c_now = -upper / denom  171 us
    all_to_all x1, blocking collectives, per_device(): lax.all_to_all(outgoing.reshape(devices, capacity, levels), ('gx', 'gy'),...  53.1 us
    while x256, other arithmetic  47.3 us
    sub x4, other arithmetic, column_solve(): x_now = values[level] - coeffs[level][None] * x_next  26.4 us
    ppermute x8, waiting for transfers between devices, extended(): lax.ppermute(lax.slice_in_dim(block, 0, width, axis=dim), axis, backward)  24.4 us
    dynamic_slice x16, local copies, waits for them, and re-layouts, implicit_mix(): lax.map(lambda pair: column_solve(pair[0], pair[1]), (mix_blocks, tracer_...  19.8 us
    ppermute x8, starting transfers between devices, extended(): lax.ppermute(lax.slice_in_dim(block, block.shape[dim] - width, None, axis...  18.4 us
    another operation x1, loops' own time, implicit_mix(): lax.map(lambda pair: column_solve(pair[0], pair[1]), (mix_blocks, tracer_...  13.1 us
  transfers between devices with their start and end apart: 16, of which 16 were waited for; matrix products, arithmetic and copies ran while one was open for 0% of the time, Pallas kernels for 0%

commit v1 on v0

v1 whole, which is shorter than its diff:
```python
import functools

import jax
import jax.numpy as jnp
from jax import lax
from jax.experimental import pallas as pl
from jax.experimental.pallas import tpu as pltpu
from jax.sharding import PartitionSpec as P

SUBSTEPS = 4
COURANT = 0.6
HALO = 4
LANE = 128
MESH = pl.DeviceIdType.MESH
ANY = pl.BlockSpec(memory_space=pl.ANY)
VMEM = pl.BlockSpec(memory_space=pltpu.VMEM)
SMEM = pl.BlockSpec(memory_space=pltpu.SMEM)


def exchange_kernel(
    ngx, ngy, wave_ref, tracers_ref, padded_ref, total_ref, loaded, send_sem, recv_sem, load_sem
):
    gx = lax.axis_index("gx")
    gy = lax.axis_index("gy")
    rows, cols = wave_ref.shape[1:3]
    tracer_count = tracers_ref.shape[0]
    groups = total_ref.shape[0] // LANE
    east = lax.rem(gx + 1, ngx)
    west = lax.rem(gx + ngx - 1, ngx)
    loads = [
        pltpu.make_async_copy(tracers_ref.at[t], loaded.at[t], load_sem.at[t])
        for t in range(tracer_count)
    ]
    for load in loads:
        load.start()
    own = pltpu.make_async_copy(
        wave_ref,
        padded_ref.at[:, pl.ds(HALO, rows), pl.ds(8, cols), :],
        load_sem.at[tracer_count],
    )
    own.start()

    barrier = pltpu.get_barrier_semaphore()
    for there in (west, east):
        pl.semaphore_signal(barrier, inc=1, device_id=(there, gy), device_id_type=MESH)

    @pl.when(gy > 0)
    def _():
        for there in (west, gx, east):
            pl.semaphore_signal(barrier, inc=1, device_id=(there, gy - 1), device_id_type=MESH)

    @pl.when(gy < ngy - 1)
    def _():
        for there in (west, gx, east):
            pl.semaphore_signal(barrier, inc=1, device_id=(there, gy + 1), device_id_type=MESH)

    peers = 2 + jnp.where(gy > 0, 3, 0) + jnp.where(gy < ngy - 1, 3, 0)
    pl.semaphore_wait(barrier, peers)

    lon_parts = {
        -1: (pl.ds(0, 8), pl.ds(cols + 8, 8)),
        0: (pl.ds(0, cols), pl.ds(8, cols)),
        1: (pl.ds(cols - 8, 8), pl.ds(0, 8)),
    }
    lat_parts = {
        -1: (pl.ds(0, HALO), pl.ds(rows + HALO, HALO)),
        0: (pl.ds(0, rows), pl.ds(HALO, rows)),
        1: (pl.ds(rows - HALO, HALO), pl.ds(0, HALO)),
    }
    lon_device = {-1: west, 0: gx, 1: east}

    def copy_to(dy, dx):
        index = (dy + 1) * 3 + dx + 1
        lat_from, lat_to = lat_parts[dy]
        lon_from, lon_to = lon_parts[dx]
        return pltpu.make_async_remote_copy(
            src_ref=wave_ref.at[:, lat_from, lon_from, :],
            dst_ref=padded_ref.at[:, lat_to, lon_to, :],
            send_sem=send_sem.at[index],
            recv_sem=recv_sem.at[index],
            device_id=(lon_device[dx], gy + dy),
            device_id_type=MESH,
        )

    @pl.when(gy > 0)
    def _():
        for dx in (0, -1, 1):
            copy_to(-1, dx).start()

    @pl.when(gy < ngy - 1)
    def _():
        for dx in (0, -1, 1):
            copy_to(1, dx).start()

    for dx in (-1, 1):
        copy_to(0, dx).start()

    for load in loads:
        load.wait()

    def transpose_group(b, carry):
        part = pl.ds(pl.multiple_of(b * LANE, LANE), LANE)
        value = loaded[0, part, :]
        for t in range(1, tracer_count):
            value = value + loaded[t, part, :]
        total_ref[pl.ds(b, LANE, stride=groups), :] = value.T
        return carry

    lax.fori_loop(0, groups, transpose_group, 0)
    own.wait()
    for dx in (-1, 1):
        copy_to(0, dx).wait()

    @pl.when(gy > 0)
    def _():
        for dx in (0, -1, 1):
            copy_to(-1, dx).wait_send()
            copy_to(1, dx).wait_recv()

    @pl.when(gy < ngy - 1)
    def _():
        for dx in (0, -1, 1):
            copy_to(1, dx).wait_send()
            copy_to(-1, dx).wait_recv()


def column_kernel(
    ngy,
    padded_ref,
    eddy_ref,
    class_ref,
    slot_ref,
    total_ref,
    wave_ref,
    mix_ref,
    inverse_ref,
    outgoing_ref,
    field,
    change,
    solved,
    sem,
):
    gy = lax.axis_index("gy")
    rows, cols, levels = eddy_ref.shape
    groups = rows * cols // LANE
    per_group = LANE // cols
    wide = cols + 16
    load = pltpu.make_async_copy(padded_ref, field.at[:, :, pl.ds(8, wide), :], sem)
    load.start()
    outgoing_ref[...] = jnp.zeros_like(outgoing_ref)
    load.wait()

    @pl.when(gy == 0)
    def _():
        field[:, pl.ds(0, HALO)] = jnp.zeros((3, HALO, wide + 16, levels), jnp.float32)

    @pl.when(gy == ngy - 1)
    def _():
        field[:, pl.ds(rows + HALO, HALO)] = jnp.zeros((3, HALO, wide + 16, levels), jnp.float32)

    here = pl.ds(8, wide)
    for step in range(SUBSTEPS):
        low = jnp.where(gy == 0, HALO, step + 1)
        high = jnp.where(gy == ngy - 1, rows + HALO, rows + 2 * HALO - 1 - step)
        north_before = field[2, low - 1, here] - COURANT * (
            field[0, low, here] - field[0, low - 1, here]
        )

        def one_row(i, north_below):
            press = field[0, i, here]
            east = field[1, i, here] - COURANT * (field[0, i, pl.ds(9, wide)] - press)
            north = field[2, i, here] - COURANT * (field[0, i + 1, here] - press)
            field[1, i, here] = east
            field[2, i, here] = north
            east_below = field[1, i, pl.ds(7, wide)]
            field[0, i, here] = press - COURANT * ((east - east_below) + (north - north_below))
            return north

        lax.fori_loop(low, high, one_row, north_before)

    lane = lax.broadcasted_iota(jnp.int32, (cols, levels), 1)
    own = pl.ds(16, cols)

    def one_group(b, carry):
        parts = []
        for r in range(per_group):
            i = b * per_group + r
            east = field[1, i + HALO, own]
            north = field[2, i + HALO, own]
            wave_ref[0, i] = field[0, i + HALO, own]
            wave_ref[1, i] = east
            wave_ref[2, i] = north
            shear = jnp.abs(pltpu.roll(east, levels - 1, 1) - east) + jnp.abs(
                pltpu.roll(north, levels - 1, 1) - north
            )
            parts.append(eddy_ref[i] * (1.0 + jnp.where(lane < levels - 1, shear, 0.0)))
        mix_ref[pl.ds(b, levels, stride=groups), :] = jnp.concatenate(parts, 0).T
        return carry

    lax.fori_loop(0, groups, one_group, 0)

    scale = 1.0 + class_ref[...].astype(jnp.float32)

    def level_rows(k):
        return pl.ds(pl.multiple_of(k * groups, groups), groups)

    def forward(k, carry):
        ratio_s, mix_below, value_below = carry
        at = level_rows(k)
        mix = jnp.where(k < levels - 1, mix_ref[at, :] * scale, 0.0)
        diagonal = 1.0 + ratio_s
        inverse = 1.0 / (diagonal + mix)
        value = (total_ref[at, :] + mix_below * value_below) * inverse
        mix_ref[at, :] = mix
        inverse_ref[at, :] = inverse
        solved[at, :] = value
        return mix * diagonal * inverse, mix, value

    zero = jnp.zeros((groups, LANE), jnp.float32)
    lax.fori_loop(0, levels, forward, (zero, zero, zero), unroll=4)

    def backward(n, above):
        at = level_rows(levels - 1 - n)
        value = solved[at, :] + mix_ref[at, :] * inverse_ref[at, :] * above
        solved[at, :] = value - total_ref[at, :]
        return value

    lax.fori_loop(0, levels, backward, zero, unroll=8)

    def back_group(b, carry):
        part = pl.ds(pl.multiple_of(b * LANE, LANE), LANE)
        change[part, :] = solved[pl.ds(b, levels, stride=groups), :].T
        return carry

    lax.fori_loop(0, groups, back_group, 0)

    def place(i, carry):
        for j in range(cols):
            outgoing_ref[pl.ds(slot_ref[i, j], 1), :] = change[pl.ds(i * cols + j, 1), :]
        return carry

    lax.fori_loop(0, rows, place, 0)


def tracer_kernel(
    ngx,
    ngy,
    tracers_ref,
    mix_hbm,
    inverse_hbm,
    outgoing_ref,
    after_ref,
    span_ref,
    loaded,
    stored,
    work,
    mix_ref,
    inverse_ref,
    send_sem,
    recv_sem,
    load_sem,
    store_sem,
    own_sem,
):
    devices = ngx * ngy
    gx = lax.axis_index("gx")
    gy = lax.axis_index("gy")
    me = gx * ngy + gy
    tracer_count, columns, levels = tracers_ref.shape
    groups = columns // LANE
    loads = [pltpu.make_async_copy(mix_hbm, mix_ref, own_sem.at[0])]
    loads.append(pltpu.make_async_copy(inverse_hbm, inverse_ref, own_sem.at[1]))
    own = pltpu.make_async_copy(outgoing_ref.at[me], span_ref.at[me], own_sem.at[2])

    def tracer_in(t):
        return pltpu.make_async_copy(tracers_ref.at[t], loaded.at[t], load_sem.at[t])

    def tracer_out(t):
        return pltpu.make_async_copy(stored.at[t], after_ref.at[t], store_sem.at[t])

    def partner(n):
        px = lax.rem(gx + n // ngy, ngx)
        py = lax.rem(gy + lax.rem(n, ngy), ngy)
        return px, py

    barrier = pltpu.get_barrier_semaphore()

    def greet(n, carry):
        pl.semaphore_signal(barrier, inc=1, device_id=partner(n), device_id_type=MESH)
        return carry

    lax.fori_loop(1, devices, greet, 0)
    for load in loads:
        load.start()
    own.start()
    for t in range(tracer_count):
        tracer_in(t).start()
    pl.semaphore_wait(barrier, devices - 1)

    def send(n):
        px, py = partner(n)
        return pltpu.make_async_remote_copy(
            src_ref=outgoing_ref.at[px * ngy + py],
            dst_ref=span_ref.at[me],
            send_sem=send_sem.at[n],
            recv_sem=recv_sem.at[n],
            device_id=(px, py),
            device_id_type=MESH,
        )

    def start_send(n, carry):
        send(n).start()
        return carry

    lax.fori_loop(1, devices, start_send, 0)
    for load in loads:
        load.wait()
    zero = jnp.zeros((groups, LANE), jnp.float32)

    def level_rows(k):
        return pl.ds(pl.multiple_of(k * groups, groups), groups)

    def one_tracer(t, carry):
        tracer_in(t).wait()

        def turn(b, carry):
            part = pl.ds(pl.multiple_of(b * LANE, LANE), LANE)
            work[pl.ds(b, levels, stride=groups), :] = loaded[t, part, :].T
            return carry

        lax.fori_loop(0, groups, turn, 0)

        def forward(k, carry):
            mix_below, value_below = carry
            at = level_rows(k)
            value = (work[at, :] + mix_below * value_below) * inverse_ref[at, :]
            work[at, :] = value
            return mix_ref[at, :], value

        lax.fori_loop(0, levels, forward, (zero, zero), unroll=8)

        def backward(n, above):
            at = level_rows(levels - 1 - n)
            value = work[at, :] + mix_ref[at, :] * inverse_ref[at, :] * above
            work[at, :] = value
            return value

        lax.fori_loop(0, levels, backward, zero, unroll=8)

        def turn_back(b, carry):
            part = pl.ds(pl.multiple_of(b * LANE, LANE), LANE)
            stored[t, part, :] = work[pl.ds(b, levels, stride=groups), :].T
            return carry

        lax.fori_loop(0, groups, turn_back, 0)
        tracer_out(t).start()
        return carry

    lax.fori_loop(0, tracer_count, one_tracer, 0)

    for t in range(tracer_count):
        tracer_out(t).wait()
    own.wait()

    def finish(n, carry):
        send(n).wait()
        return carry

    lax.fori_loop(1, devices, finish, 0)


def per_device(ngx, ngy, wave_state, tracers, eddy, cost_class, span_slot):
    rows, cols, levels = eddy.shape
    columns = rows * cols
    groups = columns // LANE
    devices = ngx * ngy
    capacity = max(2, (2 * columns + devices - 1) // devices)
    tracer_count = tracers.shape[0]
    f32 = jnp.float32
    flat = tracers.reshape(tracer_count, columns, levels)
    turned = jax.ShapeDtypeStruct((levels * groups, LANE), f32)
    dma = pltpu.SemaphoreType.DMA
    limit = 48 * 2**20

    padded, total = pl.pallas_call(
        functools.partial(exchange_kernel, ngx, ngy),
        out_shape=(
            jax.ShapeDtypeStruct((3, rows + 2 * HALO, cols + 16, levels), f32),
            turned,
        ),
        in_specs=[ANY, ANY],
        out_specs=(ANY, VMEM),
        scratch_shapes=[
            pltpu.VMEM((tracer_count, columns, levels), f32),
            dma((9,)),
            dma((9,)),
            dma((tracer_count + 1,)),
        ],
        compiler_params=pltpu.CompilerParams(
            collective_id=0, has_side_effects=True, vmem_limit_bytes=limit
        ),
        name="exchange",
    )(wave_state, flat)

    wave_after, mix, inverse, outgoing = pl.pallas_call(
        functools.partial(column_kernel, ngy),
        out_shape=(
            jax.ShapeDtypeStruct(wave_state.shape, f32),
            turned,
            turned,
            jax.ShapeDtypeStruct((devices * capacity, levels), f32),
        ),
        in_specs=[ANY, VMEM, VMEM, SMEM, VMEM],
        out_specs=(VMEM, VMEM, VMEM, VMEM),
        scratch_shapes=[
            pltpu.VMEM((3, rows + 2 * HALO, cols + 32, levels), f32),
            pltpu.VMEM((columns, levels), f32),
            pltpu.VMEM((levels * groups, LANE), f32),
            dma(()),
        ],
        compiler_params=pltpu.CompilerParams(vmem_limit_bytes=limit),
        name="columns",
    )(padded, eddy, cost_class.reshape(groups, LANE), span_slot, total)

    after, span = pl.pallas_call(
        functools.partial(tracer_kernel, ngx, ngy),
        out_shape=(
            jax.ShapeDtypeStruct((tracer_count, columns, levels), f32),
            jax.ShapeDtypeStruct((devices, capacity, levels), f32),
        ),
        in_specs=[ANY, ANY, ANY, ANY],
        out_specs=(ANY, ANY),
        scratch_shapes=[
            pltpu.VMEM((tracer_count, columns, levels), f32),
            pltpu.VMEM((tracer_count, columns, levels), f32),
            pltpu.VMEM((levels * groups, LANE), f32),
            pltpu.VMEM((levels * groups, LANE), f32),
            pltpu.VMEM((levels * groups, LANE), f32),
            dma((devices,)),
            dma((devices,)),
            dma((tracer_count,)),
            dma((tracer_count,)),
            dma((3,)),
        ],
        compiler_params=pltpu.CompilerParams(
            collective_id=1, has_side_effects=True, vmem_limit_bytes=limit
        ),
        name="tracers",
    )(flat, mix, inverse, outgoing.reshape(devices, capacity, levels))
    return wave_after, after.reshape(tracers.shape), span[None]


def solution(mesh):
    in_specs = (
        P(None, "gy", "gx", None),
        P(None, "gy", "gx", None),
        P("gy", "gx", None),
        P("gy", "gx"),
        P("gy", "gx"),
    )
    out_specs = (
        P(None, "gy", "gx", None),
        P(None, "gy", "gx", None),
        P(("gx", "gy"), None, None, None),
    )
    return jax.shard_map(
        functools.partial(per_device, mesh.shape["gx"], mesh.shape["gy"]),
        mesh=mesh,
        in_specs=in_specs,
        out_specs=out_specs,
        check_vma=False,
    )
```

time: 449 us -> 97.6 us (0.22)
  other arithmetic: 269 us -> 0 us
  Pallas kernels: 0 us -> 86 us
  blocking collectives: 53.1 us -> 0 us
  local copies, waits for them, and re-layouts: 53.1 us -> 10.6 us
  waiting for transfers between devices: 30 us -> 0 us
  starting transfers between devices: 26.1 us -> 0 us
  loops' own time: 13.1 us -> 0 us
    div x344 -> x0, other arithmetic: 175 us -> none  [the longest x340 171 us: column_solve(): c_now = -upper / denom]
    pallas_call x0 -> x3, Pallas kernels: none -> 86 us  [the longest x1 51.9 us: per_device(): pl.pallas_call(functools.partial(tracer_kernel, ngx, ngy), out_shape=(jax...]
    all_to_all x1 -> x0, blocking collectives: 53.1 us -> none  [per_device(): lax.all_to_all(outgoing.reshape(devices, capacity, levels), ('gx', 'gy'),...]
    while x256 -> x0, other arithmetic: 47.3 us -> none
    ppermute x16 -> x0, waiting for transfers between devices: 30 us -> none  [the longest x8 24.4 us: extended(): lax.ppermute(lax.slice_in_dim(block, 0, width, axis=dim), axis, backward)]
    sub x12 -> x0, other arithmetic: 28.8 us -> none  [the longest x4 26.4 us: column_solve(): x_now = values[level] - coeffs[level][None] * x_next]
    ppermute x16 -> x0, starting transfers between devices: 26.1 us -> none  [the longest x8 18.4 us: extended(): lax.ppermute(lax.slice_in_dim(block, block.shape[dim] - width, None, axis...]
    dynamic_slice x16 -> x0, local copies, waits for them, and re-layouts: 19.8 us -> none  [implicit_mix(): lax.map(lambda pair: column_solve(pair[0], pair[1]), (mix_blocks, tracer_...]
  transfers between devices with their start and end apart: 16 -> 0, of which waited for: 16 -> 0; matrix products, arithmetic and copies ran while one was open for 0% -> 0% of each run, Pallas kernels for 0% -> 0%
where the time goes in v1:
time: 97.6 us; the launch traced here: 97.3 us
  Pallas kernels  86 us (88%)
  local copies, waits for them, and re-layouts  10.6 us (11%)
    pallas_call x1, Pallas kernels, per_device(): pl.pallas_call(functools.partial(tracer_kernel, ngx, ngy), out_shape=(jax...  51.9 us
    pallas_call x1, Pallas kernels, per_device(): pl.pallas_call(functools.partial(column_kernel, ngy), out_shape=(jax.Shap...  17.1 us
    pallas_call x1, Pallas kernels, per_device(): pl.pallas_call(functools.partial(exchange_kernel, ngx, ngy), out_shape=(j...  17 us
    unnamed x8, local copies, waits for them, and re-layouts  9.83 us

profile of v1, /device:TPU:1, one launch (start us, length us, event | category | flops | bytes accessed | tf_op | source)
XLA Modules:
  0.0 97.3 jit_solution(2318872352354348147)
XLA Ops:
  0.6 0.8 reshape.19.class_ref
  1.4 0.0 copy-start
  1.4 1.9 %copy-done = f32[3,32,64,128]{3,2,1,0:T(8,128)S(1)} copy-done((f32[3,32,64,128]{3,2,1,0:T(8,128)S(1)}, f32[3,32,64,128]{3,2,1,0:T(8,128)}, u32[]{:S(2)}) %copy-start) | copy-done | bytes 3145752
  3.3 0.0 copy-start.1
  3.3 0.0 copy-start.2
  3.3 17.0 %exchange.1 = (f32[3,40,80,128]{3,2,1,0:T(8,128)}, f32[2048,128]{1,0:T(8,128)S(1)}) custom-call(f32[3,32,64,128]{3,2,1,0:T(8,128)S(1)} %copy-done, f32[6,2048,128]{2,1,0:T(8,128)} %bitcast.5), custom_call_target="tpu_custom_call" | custom-call | tf_op jit(solution)/shard_map/exchange/pallas_call | solution.py:385
  20.4 0.0 copy-done.1
  20.4 0.0 copy-done.2
  20.4 17.1 %columns.1 = (f32[3,32,64,128]{3,2,1,0:T(8,128)}, f32[2048,128]{1,0:T(8,128)S(1)}, f32[2048,128]{1,0:T(8,128)S(1)}, f32[4096,128]{1,0:T(8,128)}) custom-call(f32[3,40,80,128]{3,2,1,0:T(8,128)} %get-tuple-element.11.padded_ref, f32[32,64,128]{2,1,0:T(8,128)S(1)} %copy-done.1, s32[16,128]{1,0:T(8,128)S(1)} %reshape.19.class_ref, s32[32,64]{1,0:T(8,128)S(1)} %copy-done.2, ...), custom_call_target="tpu_custom_call" | custom-call | tf_op jit(solution)/shard_map/columns/pallas_call | solution.py:405
  37.5 51.9 %tracers.1 = (f32[6,2048,128]{2,1,0:T(8,128)}, f32[32,128,128]{2,1,0:T(8,128)S(1)}) custom-call(f32[6,2048,128]{2,1,0:T(8,128)} %bitcast.6, f32[2048,128]{1,0:T(8,128)S(1)} %get-tuple-element.14.mix_hbm, f32[2048,128]{1,0:T(8,128)S(1)} %get-tuple-element.15.inverse_hbm, f32[32,128,128]{2,1,0:T(8,128)} %bitcast.8), custom_call_target="tpu_custom_call" | custom-call | tf_op jit(solution)/shard_map/tracers/pallas_call | solution.py:425
  89.4 6.6 %copy.10 = f32[6,32,64,128]{3,2,1,0:T(8,128)} copy(f32[6,32,64,128]{3,2,1,0:T(8,128)} %bitcast.7) | data formatting | bytes 12582912
  96.0 1.3 %copy.11 = f32[1,32,128,128]{3,2,1,0:T(8,128)} copy(f32[1,32,128,128]{3,2,1,0:T(8,128)S(1)} %bitcast.4) | data formatting | bytes 4194304
Async XLA Ops:
  1.4 1.9 %copy-start = (f32[3,32,64,128]{3,2,1,0:T(8,128)S(1)}, f32[3,32,64,128]{3,2,1,0:T(8,128)}, u32[]{:S(2)}) copy-start(f32[3,32,64,128]{3,2,1,0:T(8,128)} %wave_ref.1) | copy-start | bytes 9437188
  3.3 17.0 %copy-start.1 = (f32[32,64,128]{2,1,0:T(8,128)S(1)}, f32[32,64,128]{2,1,0:T(8,128)}, u32[]{:S(2)}) copy-start(f32[32,64,128]{2,1,0:T(8,128)} %eddy_ref.1) | copy-start | bytes 3145732
  3.3 17.1 %copy-start.2 = (s32[32,64]{1,0:T(8,128)S(1)}, s32[32,64]{1,0:T(8,128)}, u32[]{:S(2)}) copy-start(s32[32,64]{1,0:T(8,128)} %slot_ref.1) | copy-start | bytes 24580

commit v2 on v1

--- a/solution.py
+++ b/solution.py
@@ -13,6 +13,7 @@
 LANE = 128
 MESH = pl.DeviceIdType.MESH
 ANY = pl.BlockSpec(memory_space=pl.ANY)
+HBM = pl.BlockSpec(memory_space=pltpu.HBM)
 VMEM = pl.BlockSpec(memory_space=pltpu.VMEM)
 SMEM = pl.BlockSpec(memory_space=pltpu.SMEM)
 
@@ -27,18 +28,18 @@
     groups = total_ref.shape[0] // LANE
     east = lax.rem(gx + 1, ngx)
     west = lax.rem(gx + ngx - 1, ngx)
+    own = pltpu.make_async_copy(
+        wave_ref,
+        padded_ref.at[:, pl.ds(HALO, rows), pl.ds(8, cols), :],
+        load_sem.at[tracer_count],
+    )
+    own.start()
     loads = [
         pltpu.make_async_copy(tracers_ref.at[t], loaded.at[t], load_sem.at[t])
         for t in range(tracer_count)
     ]
     for load in loads:
         load.start()
-    own = pltpu.make_async_copy(
-        wave_ref,
-        padded_ref.at[:, pl.ds(HALO, rows), pl.ds(8, cols), :],
-        load_sem.at[tracer_count],
-    )
-    own.start()
 
     barrier = pltpu.get_barrier_semaphore()
     for there in (west, east):
@@ -56,16 +57,17 @@
 
     peers = 2 + jnp.where(gy > 0, 3, 0) + jnp.where(gy < ngy - 1, 3, 0)
     pl.semaphore_wait(barrier, peers)
+    own.wait()
 
     lon_parts = {
-        -1: (pl.ds(0, 8), pl.ds(cols + 8, 8)),
-        0: (pl.ds(0, cols), pl.ds(8, cols)),
-        1: (pl.ds(cols - 8, 8), pl.ds(0, 8)),
+        -1: (pl.ds(8, 8), pl.ds(cols + 8, 8)),
+        0: (pl.ds(8, cols), pl.ds(8, cols)),
+        1: (pl.ds(cols, 8), pl.ds(0, 8)),
     }
     lat_parts = {
-        -1: (pl.ds(0, HALO), pl.ds(rows + HALO, HALO)),
-        0: (pl.ds(0, rows), pl.ds(HALO, rows)),
-        1: (pl.ds(rows - HALO, HALO), pl.ds(0, HALO)),
+        -1: (pl.ds(HALO, HALO), pl.ds(rows + HALO, HALO)),
+        0: (pl.ds(HALO, rows), pl.ds(HALO, rows)),
+        1: (pl.ds(rows, HALO), pl.ds(0, HALO)),
     }
     lon_device = {-1: west, 0: gx, 1: east}
 
@@ -74,7 +76,7 @@
         lat_from, lat_to = lat_parts[dy]
         lon_from, lon_to = lon_parts[dx]
         return pltpu.make_async_remote_copy(
-            src_ref=wave_ref.at[:, lat_from, lon_from, :],
+            src_ref=padded_ref.at[:, lat_from, lon_from, :],
             dst_ref=padded_ref.at[:, lat_to, lon_to, :],
             send_sem=send_sem.at[index],
             recv_sem=recv_sem.at[index],
@@ -107,7 +109,6 @@
         return carry
 
     lax.fori_loop(0, groups, transpose_group, 0)
-    own.wait()
     for dx in (-1, 1):
         copy_to(0, dx).wait()
 
@@ -199,7 +200,8 @@
 
     lax.fori_loop(0, groups, one_group, 0)
 
-    scale = 1.0 + class_ref[...].astype(jnp.float32)
+    classes = [class_ref[pl.ds(r, groups, stride=per_group), :] for r in range(per_group)]
+    scale = 1.0 + jnp.concatenate(classes, 1).astype(jnp.float32)
 
     def level_rows(k):
         return pl.ds(pl.multiple_of(k * groups, groups), groups)
@@ -252,14 +254,12 @@
     after_ref,
     span_ref,
     loaded,
-    stored,
     work,
     mix_ref,
     inverse_ref,
     send_sem,
     recv_sem,
     load_sem,
-    store_sem,
     own_sem,
 ):
     devices = ngx * ngy
@@ -275,9 +275,6 @@
     def tracer_in(t):
         return pltpu.make_async_copy(tracers_ref.at[t], loaded.at[t], load_sem.at[t])
 
-    def tracer_out(t):
-        return pltpu.make_async_copy(stored.at[t], after_ref.at[t], store_sem.at[t])
-
     def partner(n):
         px = lax.rem(gx + n // ngy, ngx)
         py = lax.rem(gy + lax.rem(n, ngy), ngy)
@@ -349,17 +346,14 @@
 
         def turn_back(b, carry):
             part = pl.ds(pl.multiple_of(b * LANE, LANE), LANE)
-            stored[t, part, :] = work[pl.ds(b, levels, stride=groups), :].T
+            after_ref[t, part, :] = work[pl.ds(b, levels, stride=groups), :].T
             return carry
 
         lax.fori_loop(0, groups, turn_back, 0)
-        tracer_out(t).start()
         return carry
 
     lax.fori_loop(0, tracer_count, one_tracer, 0)
 
-    for t in range(tracer_count):
-        tracer_out(t).wait()
     own.wait()
 
     def finish(n, carry):
@@ -377,10 +371,11 @@
     capacity = max(2, (2 * columns + devices - 1) // devices)
     tracer_count = tracers.shape[0]
     f32 = jnp.float32
-    flat = tracers.reshape(tracer_count, columns, levels)
+    flat = pltpu.with_memory_space_constraint(tracers.reshape(tracer_count, columns, levels), pltpu.HBM)
+    wave_state = pltpu.with_memory_space_constraint(wave_state, pltpu.HBM)
     turned = jax.ShapeDtypeStruct((levels * groups, LANE), f32)
     dma = pltpu.SemaphoreType.DMA
-    limit = 48 * 2**20
+    mib = 2**20
 
     padded, total = pl.pallas_call(
         functools.partial(exchange_kernel, ngx, ngy),
@@ -388,8 +383,8 @@
             jax.ShapeDtypeStruct((3, rows + 2 * HALO, cols + 16, levels), f32),
             turned,
         ),
-        in_specs=[ANY, ANY],
-        out_specs=(ANY, VMEM),
+        in_specs=[HBM, HBM],
+        out_specs=(VMEM, VMEM),
         scratch_shapes=[
             pltpu.VMEM((tracer_count, columns, levels), f32),
             dma((9,)),
@@ -397,7 +392,7 @@
             dma((tracer_count + 1,)),
         ],
         compiler_params=pltpu.CompilerParams(
-            collective_id=0, has_side_effects=True, vmem_limit_bytes=limit
+            collective_id=0, has_side_effects=True, vmem_limit_bytes=16 * mib
         ),
         name="exchange",
     )(wave_state, flat)
@@ -418,9 +413,9 @@
             pltpu.VMEM((levels * groups, LANE), f32),
             dma(()),
         ],
-        compiler_params=pltpu.CompilerParams(vmem_limit_bytes=limit),
+        compiler_params=pltpu.CompilerParams(vmem_limit_bytes=24 * mib),
         name="columns",
-    )(padded, eddy, cost_class.reshape(groups, LANE), span_slot, total)
+    )(padded, eddy, cost_class, span_slot, total)
 
     after, span = pl.pallas_call(
         functools.partial(tracer_kernel, ngx, ngy),
@@ -428,10 +423,9 @@
             jax.ShapeDtypeStruct((tracer_count, columns, levels), f32),
             jax.ShapeDtypeStruct((devices, capacity, levels), f32),
         ),
-        in_specs=[ANY, ANY, ANY, ANY],
-        out_specs=(ANY, ANY),
+        in_specs=[HBM, ANY, ANY, ANY],
+        out_specs=(VMEM, ANY),
         scratch_shapes=[
-            pltpu.VMEM((tracer_count, columns, levels), f32),
             pltpu.VMEM((tracer_count, columns, levels), f32),
             pltpu.VMEM((levels * groups, LANE), f32),
             pltpu.VMEM((levels * groups, LANE), f32),
@@ -439,11 +433,10 @@
             dma((devices,)),
             dma((devices,)),
             dma((tracer_count,)),
-            dma((tracer_count,)),
             dma((3,)),
         ],
         compiler_params=pltpu.CompilerParams(
-            collective_id=1, has_side_effects=True, vmem_limit_bytes=limit
+            collective_id=1, has_side_effects=True, vmem_limit_bytes=17 * mib
         ),
         name="tracers",
     )(flat, mix, inverse, outgoing.reshape(devices, capacity, levels))

time: 97.6 us -> 88.6 us (0.908)
  local copies, waits for them, and re-layouts: 10.6 us -> 4.04 us
  Pallas kernels: 86 us -> 83.7 us
    unnamed x8, local copies, waits for them, and re-layouts: 9.83 us -> 4.04 us
    pallas_call x1, Pallas kernels: 17.1 us -> 14.8 us  [per_device(): pl.pallas_call(functools.partial(column_kernel, ngy), out_shape=(jax.Shap...]
where the time goes in v2:
time: 88.6 us; the launch traced here: 88.4 us
  Pallas kernels  83.7 us (94%)
  local copies, waits for them, and re-layouts  4.04 us (5%)
    pallas_call x1, Pallas kernels, per_device(): pl.pallas_call(functools.partial(tracer_kernel, ngx, ngy), out_shape=(jax...  51.9 us
    pallas_call x1, Pallas kernels, per_device(): pl.pallas_call(functools.partial(exchange_kernel, ngx, ngy), out_shape=(j...  17 us
    pallas_call x1, Pallas kernels, per_device(): pl.pallas_call(functools.partial(column_kernel, ngy), out_shape=(jax.Shap...  14.8 us
    unnamed x8, local copies, waits for them, and re-layouts  4.04 us

profile of v2, /device:TPU:1, one launch (start us, length us, event | category | flops | bytes accessed | tf_op | source)
XLA Modules:
  0.0 88.4 jit_solution(8201992816476432570)
XLA Ops:
  0.6 0.0 copy-start
  0.6 0.0 copy-start.1
  0.7 0.0 copy-start.2
  0.7 17.0 %exchange.1 = (f32[3,40,80,128]{3,2,1,0:T(8,128)S(1)}, f32[2048,128]{1,0:T(8,128)S(1)}) custom-call(f32[3,32,64,128]{3,2,1,0:T(8,128)} %wave_ref.1, f32[6,2048,128]{2,1,0:T(8,128)} %bitcast.7), custom_call_target="tpu_custom_call" | custom-call | tf_op jit(solution)/shard_map/exchange/pallas_call | solution.py:380
  17.6 0.0 copy-done
  17.6 0.0 copy-done.1
  17.7 0.0 copy-done.2
  17.7 14.8 %columns.1 = (f32[3,32,64,128]{3,2,1,0:T(8,128)}, f32[2048,128]{1,0:T(8,128)S(1)}, f32[2048,128]{1,0:T(8,128)S(1)}, f32[4096,128]{1,0:T(8,128)S(1)}) custom-call(f32[3,40,80,128]{3,2,1,0:T(8,128)S(1)} %get-tuple-element.11.padded_ref, f32[32,64,128]{2,1,0:T(8,128)S(1)} %copy-done, s32[32,64]{1,0:T(8,128)S(1)} %copy-done.1, s32[32,64]{1,0:T(8,128)S(1)} %copy-done.2, ...), custom_call_target="tpu_custom_call" | custom-call | tf_op jit(solution)/shard_map/columns/pallas_call | solution.py:400
  32.5 51.9 %tracers.1 = (f32[6,2048,128]{2,1,0:T(8,128)S(1)}, f32[32,128,128]{2,1,0:T(8,128)S(1)}) custom-call(f32[6,2048,128]{2,1,0:T(8,128)} %bitcast.8, f32[2048,128]{1,0:T(8,128)S(1)} %get-tuple-element.14.mix_hbm, f32[2048,128]{1,0:T(8,128)S(1)} %get-tuple-element.15.inverse_hbm, f32[32,128,128]{2,1,0:T(8,128)S(1)} %bitcast.5), custom_call_target="tpu_custom_call" | custom-call | tf_op jit(solution)/shard_map/tracers/pallas_call | solution.py:420
  84.4 2.7 %copy.10 = f32[6,32,64,128]{3,2,1,0:T(8,128)} copy(f32[6,32,64,128]{3,2,1,0:T(8,128)S(1)} %bitcast.4) | data formatting | bytes 12582912
  87.1 1.3 %copy.11 = f32[1,32,128,128]{3,2,1,0:T(8,128)} copy(f32[1,32,128,128]{3,2,1,0:T(8,128)S(1)} %bitcast.6) | data formatting | bytes 4194304
Async XLA Ops:
  0.6 17.0 %copy-start = (f32[32,64,128]{2,1,0:T(8,128)S(1)}, f32[32,64,128]{2,1,0:T(8,128)}, u32[]{:S(2)}) copy-start(f32[32,64,128]{2,1,0:T(8,128)} %eddy_ref.1) | copy-start | bytes 3145732
  0.6 17.0 %copy-start.1 = (s32[32,64]{1,0:T(8,128)S(1)}, s32[32,64]{1,0:T(8,128)}, u32[]{:S(2)}) copy-start(s32[32,64]{1,0:T(8,128)} %class_ref.1) | copy-start | bytes 24580
  0.7 17.0 %copy-start.2 = (s32[32,64]{1,0:T(8,128)S(1)}, s32[32,64]{1,0:T(8,128)}, u32[]{:S(2)}) copy-start(s32[32,64]{1,0:T(8,128)} %slot_ref.1) | copy-start | bytes 24580
